TPU v7x, 32 devices: a whole 2x2x4 slice. The times are simulated.
32 devices in a mesh: phase: 4 (over y, x), tile: 4 (over z), dp: 2 (over core).
Axes of the slice: x: 2, y: 2, z: 4, core: 2. Of those that a mesh axis runs over, the one named last changes fastest.
Arguments:
- camera_feats: bfloat16 [4, 2, 3, 4, 176, 128], P(None, 'dp', None, 'tile'), may hold values from -6 to 6
- backbone_w: bfloat16 [4, 1152, 128], P('phase'), may hold values from -0.1875 to 0.1875
- depth_w: bfloat16 [128, 118], replicated, may hold values from -1 to 1
- block_tile: int32 [4, 2, 1056, 1], P('phase', 'dp', 'tile'), may hold values from 0 to 3; in each aligned block of 264 rows (0 to 263, 264 to 527, ..., all dimensions but the last counted through in order) at most 264 rows name the same one
- point_slot: int32 [4, 2, 1056, 236], P('phase', 'dp', 'tile'), may hold values from 0 to 15
- block_cells: int32 [4, 2, 1056, 16], P('phase', 'dp', 'tile'), may hold values from 0 to 1024, as said below
- bev_w: bfloat16 [1152, 128], replicated, may hold values from -0.1875 to 0.1875
- cotangent: bfloat16 [4, 2, 16, 256, 128], P('phase', 'dp', 'tile'), may hold values from -6 to 6
Outputs:
- encoded: bfloat16 [4, 2, 16, 256, 128], P('phase', 'dp', 'tile')
- conv_grad: float32 [128, 1152], P('tile')
Inputs may be any that keep to these rules, and one draw needn't show every extreme that they name: `block_tile`: among the 264 blocks of one sample on one index of tile (an aligned run of rows), at most 264 name the same tile. `block_cells`: 1024 marks a slot whose cell lies outside the grid.
All inputs are finite; a program needn't handle non-finite values.
Results may differ from a plain program's by a relative error of at most 0.0085.
Values may be sent and summed in bfloat16 or wider, within the bound.
A program may use at most 64 MiB of HBM per device.

v0:
```python
import jax
import jax.numpy as jnp
from jax import lax
from jax.sharding import PartitionSpec as P

NSEG = 2
BLK = 4
BOUND = 8.0


def extended(cells, sides, width):
    for axis, dim in sides:
        count = lax.axis_size(axis)
        ends = count - 1
        head = lax.slice_in_dim(cells, 0, width, axis=dim)
        tail = lax.slice_in_dim(cells, cells.shape[dim] - width, cells.shape[dim], axis=dim)
        cells = jnp.concatenate(
            [
                lax.ppermute(tail, axis, [(i, (i + 1) % count) for i in range(ends)]),
                cells,
                lax.ppermute(head, axis, [((i + 1) % count, i) for i in range(ends)]),
            ],
            axis=dim,
        )
    return cells


def passed_along(block, axis, distance):
    devices = range(lax.axis_size(axis))
    route = [(i - distance, i) for i in devices if i - distance in devices]
    return lax.ppermute(block, axis, route)


def from_root(block, axis, source):
    block = jnp.where(lax.axis_index(axis) == source, block, jnp.zeros_like(block))
    return lax.psum(block, axis)


def patches_from(padded, row_count, col_count):
    widened = jnp.pad(padded, [(0, 0)] * (padded.ndim - 2) + [(1, 1), (0, 0)])
    shifted = [
        widened[..., row_off : row_off + row_count, col_off : col_off + col_count, :]
        for row_off in range(3)
        for col_off in range(3)
    ]
    stacked = jnp.concatenate(shifted, axis=-1)
    return stacked.reshape(-1, stacked.shape[-1])


def section(images, weight):
    padded = extended(images, (("tile", 2),), 1)
    hidden = jnp.dot(
        patches_from(padded, images.shape[2], images.shape[3]),
        weight,
        preferred_element_type=jnp.float32,
    ).reshape(images.shape)
    return (images.astype(jnp.float32) + jax.nn.silu(hidden)).astype(jnp.bfloat16)


def body(camera_feats, backbone_w, depth_w, block_tile, point_slot, block_cells, bev_w, cotangent):
    phases = lax.axis_size("phase")
    phase_idx = lax.axis_index("phase")
    tile_count = lax.axis_size("tile")
    micro_all = camera_feats.shape[0]
    per_phase = micro_all // phases
    own_weight = backbone_w[0]
    carried = jnp.zeros_like(camera_feats[0])
    collected = jnp.zeros_like(camera_feats)
    steps_total = micro_all + phases - 1
    for step_idx in range(steps_total):
        if step_idx < micro_all:
            entering = jnp.where(phase_idx == 0, camera_feats[step_idx], carried)
        else:
            entering = carried
        leaving = section(entering, own_weight)
        finished = step_idx - (phases - 1)
        if finished >= 0:
            collected = collected.at[finished].set(
                jnp.where(phase_idx == phases - 1, leaving, collected[finished])
            )
        if step_idx + 1 < steps_total:
            carried = passed_along(leaving, "phase", 1)
    everything = from_root(collected, "phase", phases - 1)
    own_feats = lax.dynamic_slice_in_dim(everything, phase_idx * per_phase, per_phase, 0)
    samples_dev = own_feats.shape[0] * own_feats.shape[1]
    channels = own_feats.shape[-1]
    context = own_feats.reshape(samples_dev, -1, channels)
    positions = context.shape[1]
    seg_len = depth_w.shape[1] // NSEG
    slot_total = block_cells.shape[-1]
    pos_groups = positions // BLK
    block_count = pos_groups * NSEG
    logits = jnp.dot(context.reshape(-1, channels), depth_w, preferred_element_type=jnp.float32)
    depth_prob = jax.nn.softmax(BOUND * jnp.tanh(logits / BOUND), axis=-1)
    depth_blocks = (
        depth_prob.reshape(samples_dev, pos_groups, BLK, NSEG, seg_len)
        .transpose(0, 1, 3, 2, 4)
        .reshape(samples_dev, block_count, BLK, seg_len)
    )
    slot_blocks = point_slot.reshape(samples_dev, block_count, BLK, seg_len)
    splat_w = jnp.stack(
        [
            jnp.sum(
                jnp.where(slot_blocks == target, depth_blocks, jnp.zeros_like(depth_blocks)),
                axis=-1,
            )
            for target in range(slot_total)
        ],
        axis=2,
    ).astype(jnp.bfloat16)
    block_ctx = jnp.repeat(context.reshape(samples_dev, pos_groups, BLK, channels), NSEG, axis=1)
    row_count = cotangent.shape[2]
    col_count = cotangent.shape[3]
    cells_tile = row_count * col_count
    capacity = max(2, 4 * block_count // tile_count)
    targets = block_tile.reshape(samples_dev, block_count)
    member = (targets[..., None] == jnp.arange(tile_count, dtype=jnp.int32)).astype(jnp.int32)
    slot_rank = jnp.sum((jnp.cumsum(member, axis=1) - 1) * member, axis=-1)
    slot_flat = targets * capacity + slot_rank
    sample_rows = jnp.broadcast_to(
        jnp.arange(samples_dev, dtype=jnp.int32)[:, None], slot_flat.shape
    )
    send_ctx = (
        jnp.zeros((samples_dev, tile_count * capacity, BLK, channels), jnp.bfloat16)
        .at[sample_rows, slot_flat]
        .set(block_ctx)
    )
    send_weights = (
        jnp.zeros((samples_dev, tile_count * capacity, slot_total, BLK), jnp.bfloat16)
        .at[sample_rows, slot_flat]
        .set(splat_w)
    )
    send_cells = (
        jnp.full((samples_dev, tile_count * capacity, slot_total), cells_tile, jnp.int32)
        .at[sample_rows, slot_flat]
        .set(block_cells.reshape(samples_dev, block_count, slot_total))
    )
    send_ctx = send_ctx.reshape(samples_dev, tile_count, capacity, BLK, channels)
    send_weights = send_weights.reshape(samples_dev, tile_count, capacity, slot_total, BLK)
    send_cells = send_cells.reshape(samples_dev, tile_count, capacity, slot_total)
    got_ctx, got_weights, got_cells = (
        lax.all_to_all(send_ctx, "tile", split_axis=1, concat_axis=1, tiled=True),
        lax.all_to_all(send_weights, "tile", split_axis=1, concat_axis=1, tiled=True),
        lax.all_to_all(send_cells, "tile", split_axis=1, concat_axis=1, tiled=True),
    )
    pooled = jnp.einsum(
        "ankti,ankic->anktc", got_weights, got_ctx, preferred_element_type=jnp.float32
    ).astype(jnp.bfloat16)
    group_size = min(8, tile_count)
    group_count = tile_count // group_size
    group_rows = group_size * capacity * slot_total
    pooled_groups = jnp.moveaxis(
        pooled.reshape(samples_dev, group_count, group_rows, channels), 1, 0
    )
    cell_groups = jnp.moveaxis(got_cells.reshape(samples_dev, group_count, group_rows), 1, 0)
    cell_range = jnp.arange(cells_tile, dtype=jnp.int32).reshape(1, cells_tile, 1)

    def splat_group(grid_sum, pieces):
        part_pooled, part_cells = pieces
        one_hot = (part_cells[:, None, :] == cell_range).astype(jnp.bfloat16)
        grid_sum = grid_sum + jnp.einsum(
            "sxr,src->sxc", one_hot, part_pooled, preferred_element_type=jnp.float32
        )
        return (grid_sum, None)

    totals, _ = lax.scan(
        splat_group,
        jnp.zeros((samples_dev, cells_tile, channels), jnp.float32),
        (pooled_groups, cell_groups),
    )
    bev_grid = totals.astype(jnp.bfloat16).reshape(samples_dev, row_count, col_count, channels)
    padded_grid = extended(bev_grid, (("tile", 1),), 1)
    bev_patches = patches_from(padded_grid, row_count, col_count)
    mixed = jnp.dot(bev_patches, bev_w, preferred_element_type=jnp.float32)
    encoded = (
        (bev_grid.astype(jnp.float32).reshape(-1, channels) + mixed)
        .astype(jnp.bfloat16)
        .reshape(cotangent.shape)
    )
    upstream = cotangent.reshape(-1, channels)
    total_cells = (
        micro_all * cotangent.shape[1] * lax.axis_size("dp") * row_count * tile_count * col_count
    )
    grad_scale = float(total_cells) ** (-0.5)
    grad_share = lax.psum_scatter(
        grad_scale
        * lax.dot_general(
            upstream, bev_patches, (((0,), (0,)), ((), ())), preferred_element_type=jnp.float32
        ),
        "tile",
        scatter_dimension=0,
        tiled=True,
    )
    conv_grad = lax.psum(grad_share, ("phase", "dp"))
    return (encoded, conv_grad)


def solution(mesh):
    return jax.shard_map(
        body,
        mesh=mesh,
        in_specs=(
            P(None, "dp", None, "tile", None, None),
            P("phase", None, None),
            P(),
            P("phase", "dp", "tile", None),
            P("phase", "dp", "tile", None),
            P("phase", "dp", "tile", None),
            P(),
            P("phase", "dp", "tile", None, None),
        ),
        out_specs=(P("phase", "dp", "tile", None, None), P("tile", None)),
        check_vma=False,
    )
```

profile of v0, /device:TPU:0, one launch (start us, length us, event | category | flops | bytes accessed | tf_op | source)
XLA Modules:
  0.0 385.2 jit_solution(11881665665288128379)
XLA Ops:
  8.2 4.9 %collective-permute-start = (bf16[1,3,1,176,128]{4,3,1,2,0:T(8,128)(2,1)S(1)}, bf16[1,3,1,176,128]{4,3,1,2,0:T(8,128)(2,1)S(1)}, u32[]{:S(2)}, u32[]{:S(2)}) collective-permute-start(bf16[1,3,1,176,128]{4,3,1,2,0:T(8,128)(2,1)S(1)} %fusion.83), channel_id=1, source_target_pairs={{0,2},{2,4},{4,6},{1,3},{3,5},{5,7},{8,10},{10,12},{12,14},{9,11},... | collective-permute-start | bytes 405512 | tf_op jit(solution)/shard_map/ppermute | solution.py:19
  13.1 1.3 collective-permute-start.1
  15.9 4.1 %collective-permute-done.1 = bf16[1,3,1,176,128]{4,3,1,2,0:T(8,128)(2,1)S(1)} collective-permute-done((bf16[1,3,1,176,128]{4,3,1,2,0:T(8,128)(2,1)S(1)}, bf16[1,3,1,176,128]{4,3,1,2,0:T(8,128)(2,1)S(1)}, u32[]{:S(2)}, u32[]{:S(2)}) %collective-permute-start.1) | collective-permute-done | bytes 135200 | tf_op jit(solution)/shard_map/ppermute | solution.py:21
  21.8 3.4 collective-permute-start.2
  25.2 2.5 collective-permute-done.2
  27.8 3.5 collective-permute-start.3
  31.3 1.3 collective-permute-start.4
  33.8 4.4 %collective-permute-done.4 = bf16[1,3,1,176,128]{4,3,1,2,0:T(8,128)(2,1)S(1)} collective-permute-done((bf16[1,3,1,176,128]{4,3,1,2,0:T(8,128)(2,1)S(1)}, bf16[1,3,1,176,128]{4,3,1,2,0:T(8,128)(2,1)S(1)}, u32[]{:S(2)}, u32[]{:S(2)}) %collective-permute-start.4) | collective-permute-done | bytes 135200 | tf_op jit(solution)/shard_map/ppermute | solution.py:21
  39.3 4.4 %collective-permute-start.5 = (bf16[1,3,1,176,128]{4,3,1,2,0:T(8,128)(2,1)S(1)}, bf16[1,3,1,176,128]{4,3,1,2,0:T(8,128)(2,1)S(1)}, u32[]{:S(2)}, u32[]{:S(2)}) collective-permute-start(bf16[1,3,1,176,128]{4,3,1,2,0:T(8,128)(2,1)S(1)} %add_convert_fusion.5), channel_id=1, source_target_pairs={{0,8},{8,16},{16,24},{1,9},{9,17},{17,25},{2,10},{10,18},{18,26},{... | collective-permute-start | bytes 405512 | tf_op jit(solution)/shard_map/ppermute | solution.py:31
  43.7 2.5 collective-permute-done.5
  46.3 3.5 collective-permute-start.6
  49.8 1.3 collective-permute-start.7
  52.3 4.4 %collective-permute-done.7 = bf16[1,3,1,176,128]{4,3,1,2,0:T(8,128)(2,1)S(1)} collective-permute-done((bf16[1,3,1,176,128]{4,3,1,2,0:T(8,128)(2,1)S(1)}, bf16[1,3,1,176,128]{4,3,1,2,0:T(8,128)(2,1)S(1)}, u32[]{:S(2)}, u32[]{:S(2)}) %collective-permute-start.7) | collective-permute-done | bytes 135200 | tf_op jit(solution)/shard_map/ppermute | solution.py:21
  57.8 4.4 %collective-permute-start.8 = (bf16[1,3,1,176,128]{4,3,1,2,0:T(8,128)(2,1)S(1)}, bf16[1,3,1,176,128]{4,3,1,2,0:T(8,128)(2,1)S(1)}, u32[]{:S(2)}, u32[]{:S(2)}) collective-permute-start(bf16[1,3,1,176,128]{4,3,1,2,0:T(8,128)(2,1)S(1)} %add_convert_fusion.4), channel_id=1, source_target_pairs={{0,8},{8,16},{16,24},{1,9},{9,17},{17,25},{2,10},{10,18},{18,26},{... | collective-permute-start | bytes 405512 | tf_op jit(solution)/shard_map/ppermute | solution.py:31
  62.2 2.5 collective-permute-done.8
  64.8 1.3 collective-permute-start.10
  66.1 4.6 %collective-permute-start.9 = (bf16[1,3,1,176,128]{4,3,1,2,0:T(8,128)(2,1)S(1)}, bf16[1,3,1,176,128]{4,3,1,2,0:T(8,128)(2,1)S(1)}, u32[]{:S(2)}, u32[]{:S(2)}) collective-permute-start(bf16[1,3,1,176,128]{4,3,1,2,0:T(8,128)(2,1)S(1)} %fusion.57), channel_id=1, source_target_pairs={{0,2},{2,4},{4,6},{1,3},{3,5},{5,7},{8,10},{10,12},{12,14},{9,11},... | collective-permute-start | bytes 405512 | tf_op jit(solution)/shard_map/ppermute | solution.py:19
  71.7 1.5 collective-permute-done.9
  74.4 5.2 %collective-permute-start.11 = (bf16[1,3,1,176,128]{4,3,1,2,0:T(8,128)(2,1)S(1)}, bf16[1,3,1,176,128]{4,3,1,2,0:T(8,128)(2,1)S(1)}, u32[]{:S(2)}, u32[]{:S(2)}) collective-permute-start(bf16[1,3,1,176,128]{4,3,1,2,0:T(8,128)(2,1)S(1)} %get-tuple-element.92), channel_id=1, source_target_pairs={{0,8},{8,16},{16,24},{1,9},{9,17},{17,25},{2,10},{10,18},{18,26},{... | collective-permute-start | bytes 405512 | tf_op jit(solution)/shard_map/ppermute | solution.py:31
  79.6 2.5 collective-permute-done.11
  82.1 4.4 %collective-permute-start.12 = (bf16[1,3,1,176,128]{4,3,1,2,0:T(8,128)(2,1)S(1)}, bf16[1,3,1,176,128]{4,3,1,2,0:T(8,128)(2,1)S(1)}, u32[]{:S(2)}, u32[]{:S(2)}) collective-permute-start(bf16[1,3,1,176,128]{4,3,1,2,0:T(8,128)(2,1)S(1)} %collective-permute-done.11), channel_id=1, source_target_pairs={{0,2},{2,4},{4,6},{1,3},{3,5},{5,7},{8,10},{10,12},{12,14},{9,11},... | collective-permute-start | bytes 405512 | tf_op jit(solution)/shard_map/ppermute | solution.py:19
  89.0 4.4 %collective-permute-done.13 = bf16[1,3,1,176,128]{4,3,1,2,0:T(8,128)(2,1)S(1)} collective-permute-done((bf16[1,3,1,176,128]{4,3,1,2,0:T(8,128)(2,1)S(1)}, bf16[1,3,1,176,128]{4,3,1,2,0:T(8,128)(2,1)S(1)}, u32[]{:S(2)}, u32[]{:S(2)}) %collective-permute-start.13) | collective-permute-done | bytes 135200 | tf_op jit(solution)/shard_map/ppermute | solution.py:21
  94.6 5.3 %collective-permute-start.14 = (bf16[1,3,1,176,128]{4,3,1,2,0:T(8,128)(2,1)S(1)}, bf16[1,3,1,176,128]{4,3,1,2,0:T(8,128)(2,1)S(1)}, u32[]{:S(2)}, u32[]{:S(2)}) collective-permute-start(bf16[1,3,1,176,128]{4,3,1,2,0:T(8,128)(2,1)S(1)} %get-tuple-element.90), channel_id=1, source_target_pairs={{0,8},{8,16},{16,24},{1,9},{9,17},{17,25},{2,10},{10,18},{18,26},{... | collective-permute-start | bytes 405512 | tf_op jit(solution)/shard_map/ppermute | solution.py:31
  99.9 2.5 collective-permute-done.14
  102.4 1.9 collective-permute-start.15
  104.3 1.3 collective-permute-start.16
  107.1 4.1 %collective-permute-done.16 = bf16[1,3,1,176,128]{4,3,1,2,0:T(8,128)(2,1)S(1)} collective-permute-done((bf16[1,3,1,176,128]{4,3,1,2,0:T(8,128)(2,1)S(1)}, bf16[1,3,1,176,128]{4,3,1,2,0:T(8,128)(2,1)S(1)}, u32[]{:S(2)}, u32[]{:S(2)}) %collective-permute-start.16) | collective-permute-done | bytes 135200 | tf_op jit(solution)/shard_map/ppermute | solution.py:21
  112.4 5.3 %collective-permute-start.17 = (bf16[1,3,1,176,128]{4,3,1,2,0:T(8,128)(2,1)S(1)}, bf16[1,3,1,176,128]{4,3,1,2,0:T(8,128)(2,1)S(1)}, u32[]{:S(2)}, u32[]{:S(2)}) collective-permute-start(bf16[1,3,1,176,128]{4,3,1,2,0:T(8,128)(2,1)S(1)} %get-tuple-element.88), channel_id=1, source_target_pairs={{0,8},{8,16},{16,24},{1,9},{9,17},{17,25},{2,10},{10,18},{18,26},{... | collective-permute-start | bytes 405512 | tf_op jit(solution)/shard_map/ppermute | solution.py:31
  117.7 2.5 collective-permute-done.17
  120.2 1.9 collective-permute-start.18
  124.7 4.4 %collective-permute-done.19 = bf16[1,3,1,176,128]{4,3,1,2,0:T(8,128)(2,1)S(1)} collective-permute-done((bf16[1,3,1,176,128]{4,3,1,2,0:T(8,128)(2,1)S(1)}, bf16[1,3,1,176,128]{4,3,1,2,0:T(8,128)(2,1)S(1)}, u32[]{:S(2)}, u32[]{:S(2)}) %collective-permute-start.19) | collective-permute-done | bytes 135200 | tf_op jit(solution)/shard_map/ppermute | solution.py:21
  133.5 3.5 all-to-all-start
  141.2 36.8 %all-reduce.14.cloned.1.call-done = bf16[4,1,3,1,176,128]{5,4,2,3,1,0:T(8,128)(2,1)} async-done(((bf16[4,1,3,1,176,128]{5,4,2,3,1,0:T(8,128)(2,1)}), bf16[4,1,3,1,176,128]{5,4,2,3,1,0:T(8,128)(2,1)}) %all-reduce.14.cloned.1.call-update) | async-done | bytes 540688 | tf_op jit(solution)/shard_map/psum | solution.py:36
  180.1 7.7 %fusion.26 = (bf16[132,2,4]{2,1,0:T(2,128)(2,1)S(1)}, bf16[132,2,4]{2,1,0:T(2,128)(2,1)S(1)}, bf16[132,2,4]{2,1,0:T(2,128)(2,1)S(1)}, bf16[132,2,4]{2,1,0:T(2,12...) fusion(pred[1,132,2,4,59]{4,3,2,1,0:T(4,128)(4,1)S(1)} %eq.411,, ...), kind=kLoop, calls=%fused_computation.54 | loop fusion | flops 1976832 | bytes 1279872 | tf_op jit(solution)/shard_map/reduce_sum | solution.py:103
  202.1 8.6 %scatter_fusion = bf16[1056,16,4]{1,2,0:T(4,128)(2,1)S(1)} fusion(bf16[1056,16,4]{1,2,0:T(4,128)(2,1)S(1)} %broadcast.618, s32[264]{0:T(512)S(1)} %fusion.62, bf16[264,16,4]{1,2,0:T(4,128)(2,1)S(1)} %copy.70), kind=kCustom, calls=%fused_computation.1 | custom fusion | bytes 102432 | tf_op jit(solution)/shard_map/scatter | solution.py:131
  212.0 4.6 %all-to-all-start.1 = ((bf16[1,4,264,16,4]{2,3,4,0,1:T(8,128)(2,1)}), bf16[1,4,264,16,4]{2,3,4,0,1:T(8,128)(2,1)S(1)}, u32[]{:S(2)}, u32[]{:S(2)}) async-start(bf16[1,4,264,16,4]{2,3,4,0,1:T(8,128)(2,1)} %copy.71), calls=%async_computation.1 | async-start | bytes 393216 | tf_op jit(solution)/shard_map/all_to_all | solution.py:143
  217.8 26.7 %scatter_fusion.1 = bf16[1056,4,128]{2,1,0:T(4,128)(2,1)} fusion(bf16[1056,4,128]{2,1,0:T(4,128)(2,1)} %broadcast.620, s32[264]{0:T(512)S(1)} %fusion.62, bf16[264,4,128]{2,1,0:T(4,128)(2,1)S(1)} %bitcast.272), kind=kCustom, calls=%fused_computation.2 | custom fusion | bytes 812064 | tf_op jit(solution)/shard_map/scatter | solution.py:126
  244.6 5.1 %all-to-all-start.2 = ((bf16[1,4,264,4,128]{4,3,2,0,1:T(4,128)(2,1)}), bf16[1,4,264,4,128]{4,3,2,0,1:T(4,128)(2,1)S(1)}, u32[]{:S(2)}, u32[]{:S(2)}) async-start(bf16[1,4,264,4,128]{4,3,2,0,1:T(4,128)(2,1)} %bitcast.70), calls=%async_computation.2 | async-start | bytes 2162688 | tf_op jit(solution)/shard_map/all_to_all | solution.py:142
  250.8 24.5 %all-to-all-done.2 = bf16[1,4,264,4,128]{4,3,2,0,1:T(4,128)(2,1)S(1)} async-done(((bf16[1,4,264,4,128]{4,3,2,0,1:T(4,128)(2,1)}), bf16[1,4,264,4,128]{4,3,2,0,1:T(4,128)(2,1)S(1)}, u32[]{:S(2)}, u32[]{:S(2)}) %all-to-all-start.2) | async-done | bytes 1081376 | tf_op jit(solution)/shard_map/all_to_all | solution.py:142
  275.2 1.8 convolution_convert_fusion
  277.0 10.5 %fusion.4 = bf16[1024,128]{1,0:T(8,128)(2,1)S(1)} fusion(bf16[16896,128]{1,0:T(8,128)(2,1)S(1)} %bitcast.247, s32[16896]{0:T(1024)S(1)} %eq.358), kind=kOutput, calls=%fused_computation.15 | convolution fusion | flops 4446617600 | bytes 4655104 | tf_op jit(solution)/shard_map/while/body/eval_jaxpr/sxr,src->sxc/dot_general | solution.py:161
  287.6 1.3 collective-permute-start.20
  290.8 4.3 %collective-permute-done.21 = bf16[1,1,256,128]{3,2,1,0:T(8,128)(2,1)S(1)} collective-permute-done((bf16[1,1,256,128]{3,2,1,0:T(8,128)(2,1)S(1)}, bf16[1,1,256,128]{3,2,1,0:T(8,128)(2,1)S(1)}, u32[]{:S(2)}, u32[]{:S(2)}) %collective-permute-start.21) | collective-permute-done | bytes 65568 | tf_op jit(solution)/shard_map/ppermute | solution.py:21
  298.7 21.6 %reduce-scatter.4.cloned.1.call-done = f32[32,1152]{1,0:T(8,128)} async-done(((f32[128,1152]{1,0:T(8,128)}), f32[32,1152]{1,0:T(8,128)}) %reduce-scatter.4.cloned.1.call-update) | async-done | bytes 147472
  320.3 2.0 copy.76
  322.3 1.5 fusion.3
  323.7 53.0 %all-reduce.16.cloned.1.call-done = f32[32,1152]{0,1:T(8,128)} async-done(((f32[32,1152]{0,1:T(8,128)}), f32[32,1152]{0,1:T(8,128)}) %all-reduce.16.cloned.1.call-update) | async-done | bytes 147472 | tf_op jit(solution)/shard_map/psum | solution.py:194
  376.7 1.9 copy.73
  (208 shorter events, 53.5 us)
Async XLA Ops:
  7.2 13.6 %copy-start = (bf16[1,1152,128]{2,1,0:T(8,128)(2,1)S(1)}, bf16[1,1152,128]{2,1,0:T(8,128)(2,1)}, u32[]{:S(2)}) copy-start(bf16[1,1152,128]{2,1,0:T(8,128)(2,1)} %param.17) | copy-start | bytes 884740
  7.2 170.8 %all-reduce.14.cloned.1.call-start = ((), (), s32[]{:S(2)}) async-start(), calls=%async_computation.4 | async-start | bytes 1081344 | tf_op jit(solution)/shard_map/psum | solution.py:36
  8.2 7.8 %collective-permute-start = (bf16[1,3,1,176,128]{4,3,1,2,0:T(8,128)(2,1)S(1)}, bf16[1,3,1,176,128]{4,3,1,2,0:T(8,128)(2,1)S(1)}, u32[]{:S(2)}, u32[]{:S(2)}) collective-permute-start(bf16[1,3,1,176,128]{4,3,1,2,0:T(8,128)(2,1)S(1)} %fusion.83), channel_id=1, source_target_pairs={{0,2},{2,4},{4,6},{1,3},{3,5},{5,7},{8,10},{10,12},{12,14},{9,11},... | collective-permute-start | bytes 405512 | tf_op jit(solution)/shard_map/ppermute | solution.py:19
  13.1 6.9 %collective-permute-start.1 = (bf16[1,3,1,176,128]{4,3,1,2,0:T(8,128)(2,1)S(1)}, bf16[1,3,1,176,128]{4,3,1,2,0:T(8,128)(2,1)S(1)}, u32[]{:S(2)}, u32[]{:S(2)}) collective-permute-start(bf16[1,3,1,176,128]{4,3,1,2,0:T(8,128)(2,1)S(1)} %fusion.83), channel_id=1, source_target_pairs={{2,0},{4,2},{6,4},{3,1},{5,3},{7,5},{10,8},{12,10},{14,12},{11,9},... | collective-permute-start | bytes 405512 | tf_op jit(solution)/shard_map/ppermute | solution.py:21
  20.7 1.1 copy-start.1
  21.8 5.9 %collective-permute-start.2 = (bf16[1,3,1,176,128]{4,3,1,2,0:T(8,128)(2,1)S(1)}, bf16[1,3,1,176,128]{4,3,1,2,0:T(8,128)(2,1)S(1)}, u32[]{:S(2)}, u32[]{:S(2)}) collective-permute-start(bf16[1,3,1,176,128]{4,3,1,2,0:T(8,128)(2,1)S(1)} %add_convert_fusion.6), channel_id=1, source_target_pairs={{0,8},{8,16},{16,24},{1,9},{9,17},{17,25},{2,10},{10,18},{18,26},{... | collective-permute-start | bytes 405512 | tf_op jit(solution)/shard_map/ppermute | solution.py:31
  27.8 6.0 %collective-permute-start.3 = (bf16[1,3,1,176,128]{4,3,1,2,0:T(8,128)(2,1)S(1)}, bf16[1,3,1,176,128]{4,3,1,2,0:T(8,128)(2,1)S(1)}, u32[]{:S(2)}, u32[]{:S(2)}) collective-permute-start(bf16[1,3,1,176,128]{4,3,1,2,0:T(8,128)(2,1)S(1)} %fusion.56), channel_id=1, source_target_pairs={{0,2},{2,4},{4,6},{1,3},{3,5},{5,7},{8,10},{10,12},{12,14},{9,11},... | collective-permute-start | bytes 405512 | tf_op jit(solution)/shard_map/ppermute | solution.py:19
  31.3 6.9 %collective-permute-start.4 = (bf16[1,3,1,176,128]{4,3,1,2,0:T(8,128)(2,1)S(1)}, bf16[1,3,1,176,128]{4,3,1,2,0:T(8,128)(2,1)S(1)}, u32[]{:S(2)}, u32[]{:S(2)}) collective-permute-start(bf16[1,3,1,176,128]{4,3,1,2,0:T(8,128)(2,1)S(1)} %fusion.56), channel_id=1, source_target_pairs={{2,0},{4,2},{6,4},{3,1},{5,3},{7,5},{10,8},{12,10},{14,12},{11,9},... | collective-permute-start | bytes 405512 | tf_op jit(solution)/shard_map/ppermute | solution.py:21
  39.3 6.9 %collective-permute-start.5 = (bf16[1,3,1,176,128]{4,3,1,2,0:T(8,128)(2,1)S(1)}, bf16[1,3,1,176,128]{4,3,1,2,0:T(8,128)(2,1)S(1)}, u32[]{:S(2)}, u32[]{:S(2)}) collective-permute-start(bf16[1,3,1,176,128]{4,3,1,2,0:T(8,128)(2,1)S(1)} %add_convert_fusion.5), channel_id=1, source_target_pairs={{0,8},{8,16},{16,24},{1,9},{9,17},{17,25},{2,10},{10,18},{18,26},{... | collective-permute-start | bytes 405512 | tf_op jit(solution)/shard_map/ppermute | solution.py:31
  46.3 6.0 %collective-permute-start.6 = (bf16[1,3,1,176,128]{4,3,1,2,0:T(8,128)(2,1)S(1)}, bf16[1,3,1,176,128]{4,3,1,2,0:T(8,128)(2,1)S(1)}, u32[]{:S(2)}, u32[]{:S(2)}) collective-permute-start(bf16[1,3,1,176,128]{4,3,1,2,0:T(8,128)(2,1)S(1)} %bitcast_select_fusion.16), channel_id=1, source_target_pairs={{0,2},{2,4},{4,6},{1,3},{3,5},{5,7},{8,10},{10,12},{12,14},{9,11},... | collective-permute-start | bytes 405512 | tf_op jit(solution)/shard_map/ppermute | solution.py:19
  49.8 6.9 %collective-permute-start.7 = (bf16[1,3,1,176,128]{4,3,1,2,0:T(8,128)(2,1)S(1)}, bf16[1,3,1,176,128]{4,3,1,2,0:T(8,128)(2,1)S(1)}, u32[]{:S(2)}, u32[]{:S(2)}) collective-permute-start(bf16[1,3,1,176,128]{4,3,1,2,0:T(8,128)(2,1)S(1)} %bitcast_select_fusion.16), channel_id=1, source_target_pairs={{2,0},{4,2},{6,4},{3,1},{5,3},{7,5},{10,8},{12,10},{14,12},{11,9},... | collective-permute-start | bytes 405512 | tf_op jit(solution)/shard_map/ppermute | solution.py:21
  57.8 6.9 %collective-permute-start.8 = (bf16[1,3,1,176,128]{4,3,1,2,0:T(8,128)(2,1)S(1)}, bf16[1,3,1,176,128]{4,3,1,2,0:T(8,128)(2,1)S(1)}, u32[]{:S(2)}, u32[]{:S(2)}) collective-permute-start(bf16[1,3,1,176,128]{4,3,1,2,0:T(8,128)(2,1)S(1)} %add_convert_fusion.4), channel_id=1, source_target_pairs={{0,8},{8,16},{16,24},{1,9},{9,17},{17,25},{2,10},{10,18},{18,26},{... | collective-permute-start | bytes 405512 | tf_op jit(solution)/shard_map/ppermute | solution.py:31
  64.8 6.9 %collective-permute-start.10 = (bf16[1,3,1,176,128]{4,3,1,2,0:T(8,128)(2,1)S(1)}, bf16[1,3,1,176,128]{4,3,1,2,0:T(8,128)(2,1)S(1)}, u32[]{:S(2)}, u32[]{:S(2)}) collective-permute-start(bf16[1,3,1,176,128]{4,3,1,2,0:T(8,128)(2,1)S(1)} %fusion.57), channel_id=1, source_target_pairs={{2,0},{4,2},{6,4},{3,1},{5,3},{7,5},{10,8},{12,10},{14,12},{11,9},... | collective-permute-start | bytes 405512 | tf_op jit(solution)/shard_map/ppermute | solution.py:21
  66.1 7.1 %collective-permute-start.9 = (bf16[1,3,1,176,128]{4,3,1,2,0:T(8,128)(2,1)S(1)}, bf16[1,3,1,176,128]{4,3,1,2,0:T(8,128)(2,1)S(1)}, u32[]{:S(2)}, u32[]{:S(2)}) collective-permute-start(bf16[1,3,1,176,128]{4,3,1,2,0:T(8,128)(2,1)S(1)} %fusion.57), channel_id=1, source_target_pairs={{0,2},{2,4},{4,6},{1,3},{3,5},{5,7},{8,10},{10,12},{12,14},{9,11},... | collective-permute-start | bytes 405512 | tf_op jit(solution)/shard_map/ppermute | solution.py:19
  74.4 7.7 %collective-permute-start.11 = (bf16[1,3,1,176,128]{4,3,1,2,0:T(8,128)(2,1)S(1)}, bf16[1,3,1,176,128]{4,3,1,2,0:T(8,128)(2,1)S(1)}, u32[]{:S(2)}, u32[]{:S(2)}) collective-permute-start(bf16[1,3,1,176,128]{4,3,1,2,0:T(8,128)(2,1)S(1)} %get-tuple-element.92), channel_id=1, source_target_pairs={{0,8},{8,16},{16,24},{1,9},{9,17},{17,25},{2,10},{10,18},{18,26},{... | collective-permute-start | bytes 405512 | tf_op jit(solution)/shard_map/ppermute | solution.py:31
  82.1 6.9 %collective-permute-start.12 = (bf16[1,3,1,176,128]{4,3,1,2,0:T(8,128)(2,1)S(1)}, bf16[1,3,1,176,128]{4,3,1,2,0:T(8,128)(2,1)S(1)}, u32[]{:S(2)}, u32[]{:S(2)}) collective-permute-start(bf16[1,3,1,176,128]{4,3,1,2,0:T(8,128)(2,1)S(1)} %collective-permute-done.11), channel_id=1, source_target_pairs={{0,2},{2,4},{4,6},{1,3},{3,5},{5,7},{8,10},{10,12},{12,14},{9,11},... | collective-permute-start | bytes 405512 | tf_op jit(solution)/shard_map/ppermute | solution.py:19
  86.5 6.9 %collective-permute-start.13 = (bf16[1,3,1,176,128]{4,3,1,2,0:T(8,128)(2,1)S(1)}, bf16[1,3,1,176,128]{4,3,1,2,0:T(8,128)(2,1)S(1)}, u32[]{:S(2)}, u32[]{:S(2)}) collective-permute-start(bf16[1,3,1,176,128]{4,3,1,2,0:T(8,128)(2,1)S(1)} %collective-permute-done.11), channel_id=1, source_target_pairs={{2,0},{4,2},{6,4},{3,1},{5,3},{7,5},{10,8},{12,10},{14,12},{11,9},... | collective-permute-start | bytes 405512 | tf_op jit(solution)/shard_map/ppermute | solution.py:21
  93.9 5.9 %copy-start.6 = (s32[1,1,264,1]{2,3,1,0:T(1,128)S(1)}, s32[1,1,264,1]{2,3,1,0:T(1,128)}, u32[]{:S(2)}) copy-start(s32[1,1,264,1]{2,3,1,0:T(1,128)} %param.19) | copy-start | bytes 3172
  94.6 7.8 %collective-permute-start.14 = (bf16[1,3,1,176,128]{4,3,1,2,0:T(8,128)(2,1)S(1)}, bf16[1,3,1,176,128]{4,3,1,2,0:T(8,128)(2,1)S(1)}, u32[]{:S(2)}, u32[]{:S(2)}) collective-permute-start(bf16[1,3,1,176,128]{4,3,1,2,0:T(8,128)(2,1)S(1)} %get-tuple-element.90), channel_id=1, source_target_pairs={{0,8},{8,16},{16,24},{1,9},{9,17},{17,25},{2,10},{10,18},{18,26},{... | collective-permute-start | bytes 405512 | tf_op jit(solution)/shard_map/ppermute | solution.py:31
  102.4 4.7 %collective-permute-start.15 = (bf16[1,3,1,176,128]{4,3,1,2,0:T(8,128)(2,1)S(1)}, bf16[1,3,1,176,128]{4,3,1,2,0:T(8,128)(2,1)S(1)}, u32[]{:S(2)}, u32[]{:S(2)}) collective-permute-start(bf16[1,3,1,176,128]{4,3,1,2,0:T(8,128)(2,1)S(1)} %collective-permute-done.14), channel_id=1, source_target_pairs={{0,2},{2,4},{4,6},{1,3},{3,5},{5,7},{8,10},{10,12},{12,14},{9,11},... | collective-permute-start | bytes 405512 | tf_op jit(solution)/shard_map/ppermute | solution.py:19
  104.3 6.9 %collective-permute-start.16 = (bf16[1,3,1,176,128]{4,3,1,2,0:T(8,128)(2,1)S(1)}, bf16[1,3,1,176,128]{4,3,1,2,0:T(8,128)(2,1)S(1)}, u32[]{:S(2)}, u32[]{:S(2)}) collective-permute-start(bf16[1,3,1,176,128]{4,3,1,2,0:T(8,128)(2,1)S(1)} %collective-permute-done.14), channel_id=1, source_target_pairs={{2,0},{4,2},{6,4},{3,1},{5,3},{7,5},{10,8},{12,10},{14,12},{11,9},... | collective-permute-start | bytes 405512 | tf_op jit(solution)/shard_map/ppermute | solution.py:21
  112.4 7.8 %collective-permute-start.17 = (bf16[1,3,1,176,128]{4,3,1,2,0:T(8,128)(2,1)S(1)}, bf16[1,3,1,176,128]{4,3,1,2,0:T(8,128)(2,1)S(1)}, u32[]{:S(2)}, u32[]{:S(2)}) collective-permute-start(bf16[1,3,1,176,128]{4,3,1,2,0:T(8,128)(2,1)S(1)} %get-tuple-element.88), channel_id=1, source_target_pairs={{0,8},{8,16},{16,24},{1,9},{9,17},{17,25},{2,10},{10,18},{18,26},{... | collective-permute-start | bytes 405512 | tf_op jit(solution)/shard_map/ppermute | solution.py:31
  120.2 4.4 %collective-permute-start.18 = (bf16[1,3,1,176,128]{4,3,1,2,0:T(8,128)(2,1)S(1)}, bf16[1,3,1,176,128]{4,3,1,2,0:T(8,128)(2,1)S(1)}, u32[]{:S(2)}, u32[]{:S(2)}) collective-permute-start(bf16[1,3,1,176,128]{4,3,1,2,0:T(8,128)(2,1)S(1)} %collective-permute-done.17), channel_id=1, source_target_pairs={{0,2},{2,4},{4,6},{1,3},{3,5},{5,7},{8,10},{10,12},{12,14},{9,11},... | collective-permute-start | bytes 405512 | tf_op jit(solution)/shard_map/ppermute | solution.py:19
  122.2 6.9 %collective-permute-start.19 = (bf16[1,3,1,176,128]{4,3,1,2,0:T(8,128)(2,1)S(1)}, bf16[1,3,1,176,128]{4,3,1,2,0:T(8,128)(2,1)S(1)}, u32[]{:S(2)}, u32[]{:S(2)}) collective-permute-start(bf16[1,3,1,176,128]{4,3,1,2,0:T(8,128)(2,1)S(1)} %collective-permute-done.17), channel_id=1, source_target_pairs={{2,0},{4,2},{6,4},{3,1},{5,3},{7,5},{10,8},{12,10},{14,12},{11,9},... | collective-permute-start | bytes 405512 | tf_op jit(solution)/shard_map/ppermute | solution.py:21
  130.2 1.0 copy-start.5
  131.1 5.9 %copy-start.2 = (s32[1,1,264,236]{3,2,1,0:T(8,128)S(1)}, s32[1,1,264,236]{3,2,1,0:T(8,128)}, u32[]{:S(2)}) copy-start(s32[1,1,264,236]{3,2,1,0:T(8,128)} %param.20) | copy-start | bytes 747652
  133.5 78.5 %all-to-all-start = ((s32[1,4,264,16]{2,3,0,1:T(8,128)}), s32[1,4,264,16]{2,3,0,1:T(8,128)S(1)}, u32[]{:S(2)}, u32[]{:S(2)}) async-start(s32[1,4,264,16]{2,3,0,1:T(8,128)} %copy.48), calls=%async_computation | async-start | bytes 196608 | tf_op jit(solution)/shard_map/all_to_all | solution.py:144
  138.7 40.2 %copy-start.4 = (bf16[128,118]{0,1:T(8,128)(2,1)S(1)}, bf16[128,118]{0,1:T(8,128)(2,1)}, u32[]{:S(2)}) copy-start(bf16[128,118]{0,1:T(8,128)(2,1)} %param.18) | copy-start | bytes 90628
  212.0 32.5 %all-to-all-start.1 = ((bf16[1,4,264,16,4]{2,3,4,0,1:T(8,128)(2,1)}), bf16[1,4,264,16,4]{2,3,4,0,1:T(8,128)(2,1)S(1)}, u32[]{:S(2)}, u32[]{:S(2)}) async-start(bf16[1,4,264,16,4]{2,3,4,0,1:T(8,128)(2,1)} %copy.71), calls=%async_computation.1 | async-start | bytes 393216 | tf_op jit(solution)/shard_map/all_to_all | solution.py:143
  244.6 30.7 %all-to-all-start.2 = ((bf16[1,4,264,4,128]{4,3,2,0,1:T(4,128)(2,1)}), bf16[1,4,264,4,128]{4,3,2,0,1:T(4,128)(2,1)S(1)}, u32[]{:S(2)}, u32[]{:S(2)}) async-start(bf16[1,4,264,4,128]{4,3,2,0,1:T(4,128)(2,1)} %bitcast.70), calls=%async_computation.2 | async-start | bytes 2162688 | tf_op jit(solution)/shard_map/all_to_all | solution.py:142
  249.7 70.6 %reduce-scatter.4.cloned.1.call-start = ((), (), s32[]{:S(2)}) async-start(), calls=%async_computation.6 | async-start | bytes 737280
  287.6 3.2 collective-permute-start.20
  288.9 6.2 %collective-permute-start.21 = (bf16[1,1,256,128]{3,2,1,0:T(8,128)(2,1)S(1)}, bf16[1,1,256,128]{3,2,1,0:T(8,128)(2,1)S(1)}, u32[]{:S(2)}, u32[]{:S(2)}) collective-permute-start(bf16[1,1,256,128]{3,2,1,0:T(8,128)(2,1)S(1)} %get-tuple-element.124), channel_id=1, source_target_pairs={{2,0},{4,2},{6,4},{3,1},{5,3},{7,5},{10,8},{12,10},{14,12},{11,9},... | collective-permute-start | bytes 196616 | tf_op jit(solution)/shard_map/ppermute | solution.py:21
  295.8 1.0 copy-start.3
  298.6 23.6 %copy-start.7 = (bf16[1152,128]{1,0:T(8,128)(2,1)S(1)}, bf16[1152,128]{1,0:T(8,128)(2,1)}, u32[]{:S(2)}) copy-start(bf16[1152,128]{1,0:T(8,128)(2,1)} %param.22) | copy-start | bytes 884740
  298.6 78.1 %all-reduce.16.cloned.1.call-start = ((), (), s32[]{:S(2)}) async-start(), calls=%async_computation.5 | async-start | bytes 1179648 | tf_op jit(solution)/shard_map/psum | solution.py:194
Sparse Core Ops, SparseCore 0:
  131.3 46.6 all-reduce.13
  298.7 21.4 reduce-scatter.3
  323.4 53.2 all-reduce.15
where the time goes:
time: 387 us; the launch traced here: 385 us
  waiting for transfers between devices  190 us (49%)
  starting transfers between devices  77.4 us (20%)
  local copies, waits for them, and re-layouts  69.9 us (18%)
  matrix products  18.6 us (5%)
  between operations  14.9 us (4%)
  other arithmetic  14.7 us (4%)
    psum x1, waiting for transfers between devices, body(): conv_grad = lax.psum(grad_share, ('phase', 'dp'))  53 us
    psum x1, waiting for transfers between devices, from_root(): return lax.psum(block, axis)  36.8 us
    ppermute x8, waiting for transfers between devices, extended(): lax.ppermute(head, axis, [((i + 1) % count, i) for i in range(ends)])  31.1 us
    ppermute x6, starting transfers between devices, passed_along(): return lax.ppermute(block, axis, route)  27.9 us
    scatter x1, local copies, waits for them, and re-layouts, body(): send_ctx = jnp.zeros((samples_dev, tile_count * capacity, BLK, channels),...  26.7 us
    ppermute x8, starting transfers between devices, extended(): lax.ppermute(tail, axis, [(i, (i + 1) % count) for i in range(ends)])  25.9 us
    all_to_all x1, waiting for transfers between devices, body(): lax.all_to_all(send_ctx, 'tile', split_axis=1, concat_axis=1, tiled=True)  24.5 us
    unnamed x4, waiting for transfers between devices  21.6 us
  transfers between devices with their start and end apart: 28, of which 25 were waited for; matrix products, arithmetic and copies ran while one was open for 19% of the time, Pallas kernels for 0%

commit v1 on v0

--- a/solution.py
+++ b/solution.py
@@ -33,7 +33,7 @@
 
 def from_root(block, axis, source):
     block = jnp.where(lax.axis_index(axis) == source, block, jnp.zeros_like(block))
-    return lax.psum(block, axis)
+    return jnp.sum(lax.all_gather(block, axis), axis=0)
 
 
 def patches_from(padded, row_count, col_count):

time: 387 us -> 379 us (0.979)
  waiting for transfers between devices: 190 us -> 180 us
    psum x1 -> x0, waiting for transfers between devices: 36.8 us -> none  [from_root(): return lax.psum(block, axis)]
    all_gather x0 -> x1, waiting for transfers between devices: none -> 25.3 us  [from_root(): return jnp.sum(lax.all_gather(block, axis), axis=0)]
    unnamed x83 -> x84, local copies, waits for them, and re-layouts: 8.65 us -> 8.68 us
  transfers between devices with their start and end apart: 28 -> 28, of which waited for: 25 -> 26; matrix products, arithmetic and copies ran while one was open for 19% -> 20% of each run, Pallas kernels for 0% -> 0%
where the time goes in v1:
time: 379 us; the launch traced here: 377 us
  waiting for transfers between devices  180 us (47%)
  starting transfers between devices  77.4 us (20%)
  local copies, waits for them, and re-layouts  69.1 us (18%)
  matrix products  18.6 us (5%)
  other arithmetic  16.7 us (4%)
  between operations  14.9 us (4%)
    psum x1, waiting for transfers between devices, body(): conv_grad = lax.psum(grad_share, ('phase', 'dp'))  53.1 us
    ppermute x8, waiting for transfers between devices, extended(): lax.ppermute(head, axis, [((i + 1) % count, i) for i in range(ends)])  30.6 us
    ppermute x6, starting transfers between devices, passed_along(): return lax.ppermute(block, axis, route)  27.9 us
    scatter x1, local copies, waits for them, and re-layouts, body(): send_ctx = jnp.zeros((samples_dev, tile_count * capacity, BLK, channels),...  26.7 us
    ppermute x8, starting transfers between devices, extended(): lax.ppermute(tail, axis, [(i, (i + 1) % count) for i in range(ends)])  25.9 us
    all_gather x1, waiting for transfers between devices, from_root(): return jnp.sum(lax.all_gather(block, axis), axis=0)  25.3 us
    all_to_all x1, waiting for transfers between devices, body(): lax.all_to_all(send_ctx, 'tile', split_axis=1, concat_axis=1, tiled=True)  24.7 us
    unnamed x4, waiting for transfers between devices  21.4 us
  transfers between devices with their start and end apart: 28, of which 26 were waited for; matrix products, arithmetic and copies ran while one was open for 20% of the time, Pallas kernels for 0%

profile of v1, /device:TPU:0, one launch (start us, length us, event | category | flops | bytes accessed | tf_op | source)
XLA Modules:
  0.0 376.5 jit_solution(17488466689186262785)
XLA Ops:
  8.2 4.9 %collective-permute-start = (bf16[1,3,1,176,128]{4,3,1,2,0:T(8,128)(2,1)S(1)}, bf16[1,3,1,176,128]{4,3,1,2,0:T(8,128)(2,1)S(1)}, u32[]{:S(2)}, u32[]{:S(2)}) collective-permute-start(bf16[1,3,1,176,128]{4,3,1,2,0:T(8,128)(2,1)S(1)} %fusion.84), channel_id=1, source_target_pairs={{0,2},{2,4},{4,6},{1,3},{3,5},{5,7},{8,10},{10,12},{12,14},{9,11},... | collective-permute-start | bytes 405512 | tf_op jit(solution)/shard_map/ppermute | solution.py:19
  13.1 1.3 collective-permute-start.1
  15.9 4.1 %collective-permute-done.1 = bf16[1,3,1,176,128]{4,3,1,2,0:T(8,128)(2,1)S(1)} collective-permute-done((bf16[1,3,1,176,128]{4,3,1,2,0:T(8,128)(2,1)S(1)}, bf16[1,3,1,176,128]{4,3,1,2,0:T(8,128)(2,1)S(1)}, u32[]{:S(2)}, u32[]{:S(2)}) %collective-permute-start.1) | collective-permute-done | bytes 135200 | tf_op jit(solution)/shard_map/ppermute | solution.py:21
  21.8 3.4 collective-permute-start.2
  25.2 2.5 collective-permute-done.2
  27.8 3.5 collective-permute-start.3
  31.3 1.3 collective-permute-start.4
  33.8 4.4 %collective-permute-done.4 = bf16[1,3,1,176,128]{4,3,1,2,0:T(8,128)(2,1)S(1)} collective-permute-done((bf16[1,3,1,176,128]{4,3,1,2,0:T(8,128)(2,1)S(1)}, bf16[1,3,1,176,128]{4,3,1,2,0:T(8,128)(2,1)S(1)}, u32[]{:S(2)}, u32[]{:S(2)}) %collective-permute-start.4) | collective-permute-done | bytes 135200 | tf_op jit(solution)/shard_map/ppermute | solution.py:21
  39.3 4.4 %collective-permute-start.5 = (bf16[1,3,1,176,128]{4,3,1,2,0:T(8,128)(2,1)S(1)}, bf16[1,3,1,176,128]{4,3,1,2,0:T(8,128)(2,1)S(1)}, u32[]{:S(2)}, u32[]{:S(2)}) collective-permute-start(bf16[1,3,1,176,128]{4,3,1,2,0:T(8,128)(2,1)S(1)} %add_convert_fusion.5), channel_id=1, source_target_pairs={{0,8},{8,16},{16,24},{1,9},{9,17},{17,25},{2,10},{10,18},{18,26},{... | collective-permute-start | bytes 405512 | tf_op jit(solution)/shard_map/ppermute | solution.py:31
  43.7 2.5 collective-permute-done.5
  46.3 3.5 collective-permute-start.6
  49.8 1.3 collective-permute-start.7
  52.3 4.4 %collective-permute-done.7 = bf16[1,3,1,176,128]{4,3,1,2,0:T(8,128)(2,1)S(1)} collective-permute-done((bf16[1,3,1,176,128]{4,3,1,2,0:T(8,128)(2,1)S(1)}, bf16[1,3,1,176,128]{4,3,1,2,0:T(8,128)(2,1)S(1)}, u32[]{:S(2)}, u32[]{:S(2)}) %collective-permute-start.7) | collective-permute-done | bytes 135200 | tf_op jit(solution)/shard_map/ppermute | solution.py:21
  57.8 4.4 %collective-permute-start.8 = (bf16[1,3,1,176,128]{4,3,1,2,0:T(8,128)(2,1)S(1)}, bf16[1,3,1,176,128]{4,3,1,2,0:T(8,128)(2,1)S(1)}, u32[]{:S(2)}, u32[]{:S(2)}) collective-permute-start(bf16[1,3,1,176,128]{4,3,1,2,0:T(8,128)(2,1)S(1)} %add_convert_fusion.4), channel_id=1, source_target_pairs={{0,8},{8,16},{16,24},{1,9},{9,17},{17,25},{2,10},{10,18},{18,26},{... | collective-permute-start | bytes 405512 | tf_op jit(solution)/shard_map/ppermute | solution.py:31
  62.2 2.5 collective-permute-done.8
  66.1 4.6 %collective-permute-start.9 = (bf16[1,3,1,176,128]{4,3,1,2,0:T(8,128)(2,1)S(1)}, bf16[1,3,1,176,128]{4,3,1,2,0:T(8,128)(2,1)S(1)}, u32[]{:S(2)}, u32[]{:S(2)}) collective-permute-start(bf16[1,3,1,176,128]{4,3,1,2,0:T(8,128)(2,1)S(1)} %fusion.58), channel_id=1, source_target_pairs={{0,2},{2,4},{4,6},{1,3},{3,5},{5,7},{8,10},{10,12},{12,14},{9,11},... | collective-permute-start | bytes 405512 | tf_op jit(solution)/shard_map/ppermute | solution.py:19
  71.7 1.5 collective-permute-done.9
  74.4 5.2 %collective-permute-start.11 = (bf16[1,3,1,176,128]{4,3,1,2,0:T(8,128)(2,1)S(1)}, bf16[1,3,1,176,128]{4,3,1,2,0:T(8,128)(2,1)S(1)}, u32[]{:S(2)}, u32[]{:S(2)}) collective-permute-start(bf16[1,3,1,176,128]{4,3,1,2,0:T(8,128)(2,1)S(1)} %get-tuple-element.92), channel_id=1, source_target_pairs={{0,8},{8,16},{16,24},{1,9},{9,17},{17,25},{2,10},{10,18},{18,26},{... | collective-permute-start | bytes 405512 | tf_op jit(solution)/shard_map/ppermute | solution.py:31
  79.6 2.5 collective-permute-done.11
  82.1 4.4 %collective-permute-start.12 = (bf16[1,3,1,176,128]{4,3,1,2,0:T(8,128)(2,1)S(1)}, bf16[1,3,1,176,128]{4,3,1,2,0:T(8,128)(2,1)S(1)}, u32[]{:S(2)}, u32[]{:S(2)}) collective-permute-start(bf16[1,3,1,176,128]{4,3,1,2,0:T(8,128)(2,1)S(1)} %collective-permute-done.11), channel_id=1, source_target_pairs={{0,2},{2,4},{4,6},{1,3},{3,5},{5,7},{8,10},{10,12},{12,14},{9,11},... | collective-permute-start | bytes 405512 | tf_op jit(solution)/shard_map/ppermute | solution.py:19
  89.0 4.4 %collective-permute-done.13 = bf16[1,3,1,176,128]{4,3,1,2,0:T(8,128)(2,1)S(1)} collective-permute-done((bf16[1,3,1,176,128]{4,3,1,2,0:T(8,128)(2,1)S(1)}, bf16[1,3,1,176,128]{4,3,1,2,0:T(8,128)(2,1)S(1)}, u32[]{:S(2)}, u32[]{:S(2)}) %collective-permute-start.13) | collective-permute-done | bytes 135200 | tf_op jit(solution)/shard_map/ppermute | solution.py:21
  94.6 5.3 %collective-permute-start.14 = (bf16[1,3,1,176,128]{4,3,1,2,0:T(8,128)(2,1)S(1)}, bf16[1,3,1,176,128]{4,3,1,2,0:T(8,128)(2,1)S(1)}, u32[]{:S(2)}, u32[]{:S(2)}) collective-permute-start(bf16[1,3,1,176,128]{4,3,1,2,0:T(8,128)(2,1)S(1)} %get-tuple-element.90), channel_id=1, source_target_pairs={{0,8},{8,16},{16,24},{1,9},{9,17},{17,25},{2,10},{10,18},{18,26},{... | collective-permute-start | bytes 405512 | tf_op jit(solution)/shard_map/ppermute | solution.py:31
  99.8 2.5 collective-permute-done.14
  102.4 1.9 collective-permute-start.15
  106.8 4.4 %collective-permute-done.16 = bf16[1,3,1,176,128]{4,3,1,2,0:T(8,128)(2,1)S(1)} collective-permute-done((bf16[1,3,1,176,128]{4,3,1,2,0:T(8,128)(2,1)S(1)}, bf16[1,3,1,176,128]{4,3,1,2,0:T(8,128)(2,1)S(1)}, u32[]{:S(2)}, u32[]{:S(2)}) %collective-permute-start.16) | collective-permute-done | bytes 135200 | tf_op jit(solution)/shard_map/ppermute | solution.py:21
  112.4 5.3 %collective-permute-start.17 = (bf16[1,3,1,176,128]{4,3,1,2,0:T(8,128)(2,1)S(1)}, bf16[1,3,1,176,128]{4,3,1,2,0:T(8,128)(2,1)S(1)}, u32[]{:S(2)}, u32[]{:S(2)}) collective-permute-start(bf16[1,3,1,176,128]{4,3,1,2,0:T(8,128)(2,1)S(1)} %get-tuple-element.88), channel_id=1, source_target_pairs={{0,8},{8,16},{16,24},{1,9},{9,17},{17,25},{2,10},{10,18},{18,26},{... | collective-permute-start | bytes 405512 | tf_op jit(solution)/shard_map/ppermute | solution.py:31
  117.7 2.5 collective-permute-done.17
  120.2 1.9 collective-permute-start.18
  123.5 1.9 collective-permute-done.18
  125.4 3.7 collective-permute-done.19
  135.2 3.5 all-to-all-start
  142.8 25.3 %all-gather.3.cloned.1.call-done = bf16[16,1,3,1,176,128]{5,4,3,2,1,0:T(8,128)(2,1)} async-done(((bf16[4,1,3,1,176,128]{5,4,3,2,1,0:T(8,128)(2,1)}), bf16[16,1,3,1,176,128]{5,4,3,2,1,0:T(8,128)(2,1)}) %all-gather.3.cloned.1.call-update) | async-done | bytes 2162704 | tf_op jit(solution)/shard_map/all_gather | solution.py:36
  168.2 2.0 reduce.43
  171.4 7.7 %fusion.26 = (bf16[132,2,4]{2,1,0:T(2,128)(2,1)S(1)}, bf16[132,2,4]{2,1,0:T(2,128)(2,1)S(1)}, bf16[132,2,4]{2,1,0:T(2,128)(2,1)S(1)}, bf16[132,2,4]{2,1,0:T(2,12...) fusion(pred[1,132,2,4,59]{4,3,2,1,0:T(4,128)(4,1)S(1)} %eq.411,, ...), kind=kLoop, calls=%fused_computation.54 | loop fusion | flops 1976832 | bytes 1279872 | tf_op jit(solution)/shard_map/reduce_sum | solution.py:103
  193.4 8.6 %scatter_fusion = bf16[1056,16,4]{1,2,0:T(4,128)(2,1)S(1)} fusion(bf16[1056,16,4]{1,2,0:T(4,128)(2,1)S(1)} %broadcast.618, s32[264]{0:T(512)S(1)} %fusion.63, bf16[264,16,4]{1,2,0:T(4,128)(2,1)S(1)} %copy.72), kind=kCustom, calls=%fused_computation.1 | custom fusion | bytes 102432 | tf_op jit(solution)/shard_map/scatter | solution.py:131
  203.3 4.6 %all-to-all-start.1 = ((bf16[1,4,264,16,4]{2,3,4,0,1:T(8,128)(2,1)}), bf16[1,4,264,16,4]{2,3,4,0,1:T(8,128)(2,1)S(1)}, u32[]{:S(2)}, u32[]{:S(2)}) async-start(bf16[1,4,264,16,4]{2,3,4,0,1:T(8,128)(2,1)} %copy.73), calls=%async_computation.1 | async-start | bytes 393216 | tf_op jit(solution)/shard_map/all_to_all | solution.py:143
  209.1 26.7 %scatter_fusion.1 = bf16[1056,4,128]{2,1,0:T(4,128)(2,1)} fusion(bf16[1056,4,128]{2,1,0:T(4,128)(2,1)} %broadcast.620, s32[264]{0:T(512)S(1)} %fusion.63, bf16[264,4,128]{2,1,0:T(4,128)(2,1)S(1)} %bitcast.280), kind=kCustom, calls=%fused_computation.2 | custom fusion | bytes 812064 | tf_op jit(solution)/shard_map/scatter | solution.py:126
  235.8 5.1 %all-to-all-start.2 = ((bf16[1,4,264,4,128]{4,3,2,0,1:T(4,128)(2,1)}), bf16[1,4,264,4,128]{4,3,2,0,1:T(4,128)(2,1)S(1)}, u32[]{:S(2)}, u32[]{:S(2)}) async-start(bf16[1,4,264,4,128]{4,3,2,0,1:T(4,128)(2,1)} %bitcast.73), calls=%async_computation.2 | async-start | bytes 2162688 | tf_op jit(solution)/shard_map/all_to_all | solution.py:142
  242.0 24.7 %all-to-all-done.2 = bf16[1,4,264,4,128]{4,3,2,0,1:T(4,128)(2,1)S(1)} async-done(((bf16[1,4,264,4,128]{4,3,2,0,1:T(4,128)(2,1)}), bf16[1,4,264,4,128]{4,3,2,0,1:T(4,128)(2,1)S(1)}, u32[]{:S(2)}, u32[]{:S(2)}) %all-to-all-start.2) | async-done | bytes 1081376 | tf_op jit(solution)/shard_map/all_to_all | solution.py:142
  266.7 1.8 convolution_convert_fusion
  268.5 10.5 %fusion.4 = bf16[1024,128]{1,0:T(8,128)(2,1)S(1)} fusion(bf16[16896,128]{1,0:T(8,128)(2,1)S(1)} %bitcast.252, s32[16896]{0:T(1024)S(1)} %eq.358), kind=kOutput, calls=%fused_computation.15 | convolution fusion | flops 4446617600 | bytes 4655104 | tf_op jit(solution)/shard_map/while/body/eval_jaxpr/sxr,src->sxc/dot_general | solution.py:161
  279.0 1.3 collective-permute-start.20
  282.2 4.3 %collective-permute-done.21 = bf16[1,1,256,128]{3,2,1,0:T(8,128)(2,1)S(1)} collective-permute-done((bf16[1,1,256,128]{3,2,1,0:T(8,128)(2,1)S(1)}, bf16[1,1,256,128]{3,2,1,0:T(8,128)(2,1)S(1)}, u32[]{:S(2)}, u32[]{:S(2)}) %collective-permute-start.21) | collective-permute-done | bytes 65568 | tf_op jit(solution)/shard_map/ppermute | solution.py:21
  290.1 21.3 %reduce-scatter.4.cloned.1.call-done = f32[32,1152]{1,0:T(8,128)} async-done(((f32[128,1152]{1,0:T(8,128)}), f32[32,1152]{1,0:T(8,128)}) %reduce-scatter.4.cloned.1.call-update) | async-done | bytes 147472
  311.5 2.0 copy.78
  313.5 1.5 fusion.3
  314.9 53.1 %all-reduce.13.cloned.1.call-done = f32[32,1152]{0,1:T(8,128)} async-done(((f32[32,1152]{0,1:T(8,128)}), f32[32,1152]{0,1:T(8,128)}) %all-reduce.13.cloned.1.call-update) | async-done | bytes 147472 | tf_op jit(solution)/shard_map/psum | solution.py:194
  368.0 1.9 copy.75
  (210 shorter events, 55.4 us)
Async XLA Ops:
  7.2 13.6 %copy-start = (bf16[1,1152,128]{2,1,0:T(8,128)(2,1)S(1)}, bf16[1,1152,128]{2,1,0:T(8,128)(2,1)}, u32[]{:S(2)}) copy-start(bf16[1,1152,128]{2,1,0:T(8,128)(2,1)} %param.17) | copy-start | bytes 884740
  7.2 161.0 %all-gather.3.cloned.1.call-start = ((), (), s32[]{:S(2)}) async-start(), calls=%async_computation.5 | async-start | bytes 2703360 | tf_op jit(solution)/shard_map/all_gather | solution.py:36
  8.2 7.8 %collective-permute-start = (bf16[1,3,1,176,128]{4,3,1,2,0:T(8,128)(2,1)S(1)}, bf16[1,3,1,176,128]{4,3,1,2,0:T(8,128)(2,1)S(1)}, u32[]{:S(2)}, u32[]{:S(2)}) collective-permute-start(bf16[1,3,1,176,128]{4,3,1,2,0:T(8,128)(2,1)S(1)} %fusion.84), channel_id=1, source_target_pairs={{0,2},{2,4},{4,6},{1,3},{3,5},{5,7},{8,10},{10,12},{12,14},{9,11},... | collective-permute-start | bytes 405512 | tf_op jit(solution)/shard_map/ppermute | solution.py:19
  13.1 6.9 %collective-permute-start.1 = (bf16[1,3,1,176,128]{4,3,1,2,0:T(8,128)(2,1)S(1)}, bf16[1,3,1,176,128]{4,3,1,2,0:T(8,128)(2,1)S(1)}, u32[]{:S(2)}, u32[]{:S(2)}) collective-permute-start(bf16[1,3,1,176,128]{4,3,1,2,0:T(8,128)(2,1)S(1)} %fusion.84), channel_id=1, source_target_pairs={{2,0},{4,2},{6,4},{3,1},{5,3},{7,5},{10,8},{12,10},{14,12},{11,9},... | collective-permute-start | bytes 405512 | tf_op jit(solution)/shard_map/ppermute | solution.py:21
  20.7 1.1 copy-start.1
  21.8 5.9 %collective-permute-start.2 = (bf16[1,3,1,176,128]{4,3,1,2,0:T(8,128)(2,1)S(1)}, bf16[1,3,1,176,128]{4,3,1,2,0:T(8,128)(2,1)S(1)}, u32[]{:S(2)}, u32[]{:S(2)}) collective-permute-start(bf16[1,3,1,176,128]{4,3,1,2,0:T(8,128)(2,1)S(1)} %add_convert_fusion.6), channel_id=1, source_target_pairs={{0,8},{8,16},{16,24},{1,9},{9,17},{17,25},{2,10},{10,18},{18,26},{... | collective-permute-start | bytes 405512 | tf_op jit(solution)/shard_map/ppermute | solution.py:31
  27.8 6.0 %collective-permute-start.3 = (bf16[1,3,1,176,128]{4,3,1,2,0:T(8,128)(2,1)S(1)}, bf16[1,3,1,176,128]{4,3,1,2,0:T(8,128)(2,1)S(1)}, u32[]{:S(2)}, u32[]{:S(2)}) collective-permute-start(bf16[1,3,1,176,128]{4,3,1,2,0:T(8,128)(2,1)S(1)} %fusion.56), channel_id=1, source_target_pairs={{0,2},{2,4},{4,6},{1,3},{3,5},{5,7},{8,10},{10,12},{12,14},{9,11},... | collective-permute-start | bytes 405512 | tf_op jit(solution)/shard_map/ppermute | solution.py:19
  31.3 6.9 %collective-permute-start.4 = (bf16[1,3,1,176,128]{4,3,1,2,0:T(8,128)(2,1)S(1)}, bf16[1,3,1,176,128]{4,3,1,2,0:T(8,128)(2,1)S(1)}, u32[]{:S(2)}, u32[]{:S(2)}) collective-permute-start(bf16[1,3,1,176,128]{4,3,1,2,0:T(8,128)(2,1)S(1)} %fusion.56), channel_id=1, source_target_pairs={{2,0},{4,2},{6,4},{3,1},{5,3},{7,5},{10,8},{12,10},{14,12},{11,9},... | collective-permute-start | bytes 405512 | tf_op jit(solution)/shard_map/ppermute | solution.py:21
  39.3 6.9 %collective-permute-start.5 = (bf16[1,3,1,176,128]{4,3,1,2,0:T(8,128)(2,1)S(1)}, bf16[1,3,1,176,128]{4,3,1,2,0:T(8,128)(2,1)S(1)}, u32[]{:S(2)}, u32[]{:S(2)}) collective-permute-start(bf16[1,3,1,176,128]{4,3,1,2,0:T(8,128)(2,1)S(1)} %add_convert_fusion.5), channel_id=1, source_target_pairs={{0,8},{8,16},{16,24},{1,9},{9,17},{17,25},{2,10},{10,18},{18,26},{... | collective-permute-start | bytes 405512 | tf_op jit(solution)/shard_map/ppermute | solution.py:31
  46.3 6.0 %collective-permute-start.6 = (bf16[1,3,1,176,128]{4,3,1,2,0:T(8,128)(2,1)S(1)}, bf16[1,3,1,176,128]{4,3,1,2,0:T(8,128)(2,1)S(1)}, u32[]{:S(2)}, u32[]{:S(2)}) collective-permute-start(bf16[1,3,1,176,128]{4,3,1,2,0:T(8,128)(2,1)S(1)} %fusion.57), channel_id=1, source_target_pairs={{0,2},{2,4},{4,6},{1,3},{3,5},{5,7},{8,10},{10,12},{12,14},{9,11},... | collective-permute-start | bytes 405512 | tf_op jit(solution)/shard_map/ppermute | solution.py:19
  49.8 6.9 %collective-permute-start.7 = (bf16[1,3,1,176,128]{4,3,1,2,0:T(8,128)(2,1)S(1)}, bf16[1,3,1,176,128]{4,3,1,2,0:T(8,128)(2,1)S(1)}, u32[]{:S(2)}, u32[]{:S(2)}) collective-permute-start(bf16[1,3,1,176,128]{4,3,1,2,0:T(8,128)(2,1)S(1)} %fusion.57), channel_id=1, source_target_pairs={{2,0},{4,2},{6,4},{3,1},{5,3},{7,5},{10,8},{12,10},{14,12},{11,9},... | collective-permute-start | bytes 405512 | tf_op jit(solution)/shard_map/ppermute | solution.py:21
  57.8 6.9 %collective-permute-start.8 = (bf16[1,3,1,176,128]{4,3,1,2,0:T(8,128)(2,1)S(1)}, bf16[1,3,1,176,128]{4,3,1,2,0:T(8,128)(2,1)S(1)}, u32[]{:S(2)}, u32[]{:S(2)}) collective-permute-start(bf16[1,3,1,176,128]{4,3,1,2,0:T(8,128)(2,1)S(1)} %add_convert_fusion.4), channel_id=1, source_target_pairs={{0,8},{8,16},{16,24},{1,9},{9,17},{17,25},{2,10},{10,18},{18,26},{... | collective-permute-start | bytes 405512 | tf_op jit(solution)/shard_map/ppermute | solution.py:31
  64.8 6.9 %collective-permute-start.10 = (bf16[1,3,1,176,128]{4,3,1,2,0:T(8,128)(2,1)S(1)}, bf16[1,3,1,176,128]{4,3,1,2,0:T(8,128)(2,1)S(1)}, u32[]{:S(2)}, u32[]{:S(2)}) collective-permute-start(bf16[1,3,1,176,128]{4,3,1,2,0:T(8,128)(2,1)S(1)} %fusion.58), channel_id=1, source_target_pairs={{2,0},{4,2},{6,4},{3,1},{5,3},{7,5},{10,8},{12,10},{14,12},{11,9},... | collective-permute-start | bytes 405512 | tf_op jit(solution)/shard_map/ppermute | solution.py:21
  66.1 7.1 %collective-permute-start.9 = (bf16[1,3,1,176,128]{4,3,1,2,0:T(8,128)(2,1)S(1)}, bf16[1,3,1,176,128]{4,3,1,2,0:T(8,128)(2,1)S(1)}, u32[]{:S(2)}, u32[]{:S(2)}) collective-permute-start(bf16[1,3,1,176,128]{4,3,1,2,0:T(8,128)(2,1)S(1)} %fusion.58), channel_id=1, source_target_pairs={{0,2},{2,4},{4,6},{1,3},{3,5},{5,7},{8,10},{10,12},{12,14},{9,11},... | collective-permute-start | bytes 405512 | tf_op jit(solution)/shard_map/ppermute | solution.py:19
  74.4 7.7 %collective-permute-start.11 = (bf16[1,3,1,176,128]{4,3,1,2,0:T(8,128)(2,1)S(1)}, bf16[1,3,1,176,128]{4,3,1,2,0:T(8,128)(2,1)S(1)}, u32[]{:S(2)}, u32[]{:S(2)}) collective-permute-start(bf16[1,3,1,176,128]{4,3,1,2,0:T(8,128)(2,1)S(1)} %get-tuple-element.92), channel_id=1, source_target_pairs={{0,8},{8,16},{16,24},{1,9},{9,17},{17,25},{2,10},{10,18},{18,26},{... | collective-permute-start | bytes 405512 | tf_op jit(solution)/shard_map/ppermute | solution.py:31
  82.1 6.9 %collective-permute-start.12 = (bf16[1,3,1,176,128]{4,3,1,2,0:T(8,128)(2,1)S(1)}, bf16[1,3,1,176,128]{4,3,1,2,0:T(8,128)(2,1)S(1)}, u32[]{:S(2)}, u32[]{:S(2)}) collective-permute-start(bf16[1,3,1,176,128]{4,3,1,2,0:T(8,128)(2,1)S(1)} %collective-permute-done.11), channel_id=1, source_target_pairs={{0,2},{2,4},{4,6},{1,3},{3,5},{5,7},{8,10},{10,12},{12,14},{9,11},... | collective-permute-start | bytes 405512 | tf_op jit(solution)/shard_map/ppermute | solution.py:19
  86.5 6.9 %collective-permute-start.13 = (bf16[1,3,1,176,128]{4,3,1,2,0:T(8,128)(2,1)S(1)}, bf16[1,3,1,176,128]{4,3,1,2,0:T(8,128)(2,1)S(1)}, u32[]{:S(2)}, u32[]{:S(2)}) collective-permute-start(bf16[1,3,1,176,128]{4,3,1,2,0:T(8,128)(2,1)S(1)} %collective-permute-done.11), channel_id=1, source_target_pairs={{2,0},{4,2},{6,4},{3,1},{5,3},{7,5},{10,8},{12,10},{14,12},{11,9},... | collective-permute-start | bytes 405512 | tf_op jit(solution)/shard_map/ppermute | solution.py:21
  94.6 7.8 %collective-permute-start.14 = (bf16[1,3,1,176,128]{4,3,1,2,0:T(8,128)(2,1)S(1)}, bf16[1,3,1,176,128]{4,3,1,2,0:T(8,128)(2,1)S(1)}, u32[]{:S(2)}, u32[]{:S(2)}) collective-permute-start(bf16[1,3,1,176,128]{4,3,1,2,0:T(8,128)(2,1)S(1)} %get-tuple-element.90), channel_id=1, source_target_pairs={{0,8},{8,16},{16,24},{1,9},{9,17},{17,25},{2,10},{10,18},{18,26},{... | collective-permute-start | bytes 405512 | tf_op jit(solution)/shard_map/ppermute | solution.py:31
  102.4 4.5 %collective-permute-start.15 = (bf16[1,3,1,176,128]{4,3,1,2,0:T(8,128)(2,1)S(1)}, bf16[1,3,1,176,128]{4,3,1,2,0:T(8,128)(2,1)S(1)}, u32[]{:S(2)}, u32[]{:S(2)}) collective-permute-start(bf16[1,3,1,176,128]{4,3,1,2,0:T(8,128)(2,1)S(1)} %collective-permute-done.14), channel_id=1, source_target_pairs={{0,2},{2,4},{4,6},{1,3},{3,5},{5,7},{8,10},{10,12},{12,14},{9,11},... | collective-permute-start | bytes 405512 | tf_op jit(solution)/shard_map/ppermute | solution.py:19
  104.3 6.9 %collective-permute-start.16 = (bf16[1,3,1,176,128]{4,3,1,2,0:T(8,128)(2,1)S(1)}, bf16[1,3,1,176,128]{4,3,1,2,0:T(8,128)(2,1)S(1)}, u32[]{:S(2)}, u32[]{:S(2)}) collective-permute-start(bf16[1,3,1,176,128]{4,3,1,2,0:T(8,128)(2,1)S(1)} %collective-permute-done.14), channel_id=1, source_target_pairs={{2,0},{4,2},{6,4},{3,1},{5,3},{7,5},{10,8},{12,10},{14,12},{11,9},... | collective-permute-start | bytes 405512 | tf_op jit(solution)/shard_map/ppermute | solution.py:21
  112.4 7.8 %collective-permute-start.17 = (bf16[1,3,1,176,128]{4,3,1,2,0:T(8,128)(2,1)S(1)}, bf16[1,3,1,176,128]{4,3,1,2,0:T(8,128)(2,1)S(1)}, u32[]{:S(2)}, u32[]{:S(2)}) collective-permute-start(bf16[1,3,1,176,128]{4,3,1,2,0:T(8,128)(2,1)S(1)} %get-tuple-element.88), channel_id=1, source_target_pairs={{0,8},{8,16},{16,24},{1,9},{9,17},{17,25},{2,10},{10,18},{18,26},{... | collective-permute-start | bytes 405512 | tf_op jit(solution)/shard_map/ppermute | solution.py:31
  120.2 5.2 %collective-permute-start.18 = (bf16[1,3,1,176,128]{4,3,1,2,0:T(8,128)(2,1)S(1)}, bf16[1,3,1,176,128]{4,3,1,2,0:T(8,128)(2,1)S(1)}, u32[]{:S(2)}, u32[]{:S(2)}) collective-permute-start(bf16[1,3,1,176,128]{4,3,1,2,0:T(8,128)(2,1)S(1)} %collective-permute-done.17), channel_id=1, source_target_pairs={{0,2},{2,4},{4,6},{1,3},{3,5},{5,7},{8,10},{10,12},{12,14},{9,11},... | collective-permute-start | bytes 405512 | tf_op jit(solution)/shard_map/ppermute | solution.py:19
  122.1 7.0 %collective-permute-start.19 = (bf16[1,3,1,176,128]{4,3,1,2,0:T(8,128)(2,1)S(1)}, bf16[1,3,1,176,128]{4,3,1,2,0:T(8,128)(2,1)S(1)}, u32[]{:S(2)}, u32[]{:S(2)}) collective-permute-start(bf16[1,3,1,176,128]{4,3,1,2,0:T(8,128)(2,1)S(1)} %collective-permute-done.17), channel_id=1, source_target_pairs={{2,0},{4,2},{6,4},{3,1},{5,3},{7,5},{10,8},{12,10},{14,12},{11,9},... | collective-permute-start | bytes 405512 | tf_op jit(solution)/shard_map/ppermute | solution.py:21
  130.2 1.0 copy-start.6
  130.3 2.5 copy-start.5
  131.2 7.5 %copy-start.2 = (s32[1,1,264,236]{3,2,1,0:T(8,128)S(1)}, s32[1,1,264,236]{3,2,1,0:T(8,128)}, u32[]{:S(2)}) copy-start(s32[1,1,264,236]{3,2,1,0:T(8,128)} %param.20) | copy-start | bytes 747652
  135.2 68.1 %all-to-all-start = ((s32[1,4,264,16]{2,3,0,1:T(8,128)}), s32[1,4,264,16]{2,3,0,1:T(8,128)S(1)}, u32[]{:S(2)}, u32[]{:S(2)}) async-start(s32[1,4,264,16]{2,3,0,1:T(8,128)} %copy.48), calls=%async_computation | async-start | bytes 196608 | tf_op jit(solution)/shard_map/all_to_all | solution.py:144
  168.2 2.0 copy-start.4
  203.3 32.5 %all-to-all-start.1 = ((bf16[1,4,264,16,4]{2,3,4,0,1:T(8,128)(2,1)}), bf16[1,4,264,16,4]{2,3,4,0,1:T(8,128)(2,1)S(1)}, u32[]{:S(2)}, u32[]{:S(2)}) async-start(bf16[1,4,264,16,4]{2,3,4,0,1:T(8,128)(2,1)} %copy.73), calls=%async_computation.1 | async-start | bytes 393216 | tf_op jit(solution)/shard_map/all_to_all | solution.py:143
  235.8 30.9 %all-to-all-start.2 = ((bf16[1,4,264,4,128]{4,3,2,0,1:T(4,128)(2,1)}), bf16[1,4,264,4,128]{4,3,2,0,1:T(4,128)(2,1)S(1)}, u32[]{:S(2)}, u32[]{:S(2)}) async-start(bf16[1,4,264,4,128]{4,3,2,0,1:T(4,128)(2,1)} %bitcast.73), calls=%async_computation.2 | async-start | bytes 2162688 | tf_op jit(solution)/shard_map/all_to_all | solution.py:142
  240.9 70.5 %reduce-scatter.4.cloned.1.call-start = ((), (), s32[]{:S(2)}) async-start(), calls=%async_computation.6 | async-start | bytes 737280
  279.0 3.2 collective-permute-start.20
  280.3 6.2 %collective-permute-start.21 = (bf16[1,1,256,128]{3,2,1,0:T(8,128)(2,1)S(1)}, bf16[1,1,256,128]{3,2,1,0:T(8,128)(2,1)S(1)}, u32[]{:S(2)}, u32[]{:S(2)}) collective-permute-start(bf16[1,1,256,128]{3,2,1,0:T(8,128)(2,1)S(1)} %get-tuple-element.124), channel_id=1, source_target_pairs={{2,0},{4,2},{6,4},{3,1},{5,3},{7,5},{10,8},{12,10},{14,12},{11,9},... | collective-permute-start | bytes 196616 | tf_op jit(solution)/shard_map/ppermute | solution.py:21
  287.2 1.0 copy-start.3
  290.1 23.4 %copy-start.7 = (bf16[1152,128]{1,0:T(8,128)(2,1)S(1)}, bf16[1152,128]{1,0:T(8,128)(2,1)}, u32[]{:S(2)}) copy-start(bf16[1152,128]{1,0:T(8,128)(2,1)} %param.22) | copy-start | bytes 884740
  290.1 78.0 %all-reduce.13.cloned.1.call-start = ((), (), s32[]{:S(2)}) async-start(), calls=%async_computation.4 | async-start | bytes 1179648 | tf_op jit(solution)/shard_map/psum | solution.py:194
Sparse Core Ops, SparseCore 0:
  131.4 36.7 all-gather.2
  290.2 21.2 reduce-scatter.3
  314.6 53.3 all-reduce.12
